TPU v7x, 256 devices: a whole 4x4x8 slice. The times are simulated.
256 devices in a mesh: vocab: 32 (over y, x, core), width: 8 (over z).
Axes of the slice: x: 4, y: 4, z: 8, core: 2. Of those that a mesh axis runs over, the one named last changes fastest.
Arguments:
- hidden: bfloat16 [512, 5376], P(None, 'width'), may hold values from -3 to 3
- weight: float32 [32768, 5376], P('vocab', 'width'), may hold values from -1.1 to 1.1, as said below
- scale: float32 [32768], P('vocab'), may hold values from 0.01 to 0.1
- flags: int32 [32768], P('vocab'), may hold values from 0 to 1
- targets: int32 [512], replicated, may hold values from 0 to 32767, as said below
Outputs:
- grad_weight: float32 [32768, 5376], P('vocab', 'width')
- grad_scale: float32 [32768], P('vocab')
- grad_hidden: float32 [512, 5376], P(None, 'width')
- loss: float32 [], replicated
Inputs may be any that keep to these rules, and one draw needn't show every extreme that they name: `targets`: no target is a padded row. weight / scale stays 0.1 or more away from every odd multiple of 0.5.
All inputs are finite; a program needn't handle non-finite values.
Results may differ from a plain program's by a relative error of at most 0.0009.
The roundings to bfloat16 on the way count: a program that leaves them out, or rounds other values in their place, can miss the bound.
Values may be sent and summed in bfloat16 or wider, within the bound.
A program may use at most 64 MiB of HBM per device.

v0:
```python
import math

import jax
import jax.numpy as jnp
from jax import lax
from jax.sharding import PartitionSpec as P

D = 5376


NEG_FILL = -1e30
DECAY = 0.1


def quantize(weight, scale):
    ratios = weight / scale[:, None]
    rounded = jnp.floor(ratios + 0.5)
    levels = jnp.clip(rounded, -8.0, 7.0)
    inside = ((rounded >= -8.0) & (rounded <= 7.0)).astype(jnp.float32)
    quantized = (scale[:, None] * levels).astype(jnp.bfloat16)
    return (ratios, levels, inside, quantized)


def softmax_rows(logits, row_targets, usable, columns):
    masked = jnp.where(usable[None, :], logits, NEG_FILL)
    local_top = jnp.max(masked, axis=1)
    onehot = columns[None, :] == row_targets[:, None]
    picked = jnp.sum(jnp.where(onehot, logits, 0.0), axis=1)
    row_top = lax.pmax(local_top, "vocab")
    exp_terms = jnp.where(usable[None, :], jnp.exp(logits - row_top[:, None]), 0.0)
    row_total, picked = lax.psum((jnp.sum(exp_terms, axis=1), picked), "vocab")
    loss_part = jnp.sum(row_top + jnp.log(row_total) - picked)
    dlogits = (exp_terms / row_total[:, None] - onehot.astype(jnp.float32)).astype(jnp.bfloat16)
    return (dlogits, loss_part)


def per_device(hidden, weight, scale, flags, targets):
    ratios, levels, inside, quantized = quantize(weight, scale)
    usable = flags == 0
    slab_rows = weight.shape[0]
    columns = lax.axis_index("vocab") * slab_rows + jnp.arange(slab_rows, dtype=jnp.int32)
    contract_width = (((1,), (1,)), ((), ()))
    contract_tokens = (((0,), (0,)), ((), ()))
    partial_value = lax.dot_general(
        hidden, quantized, contract_width, preferred_element_type=jnp.float32
    )
    logits = lax.psum(partial_value, "width")
    dlogits, loss = softmax_rows(logits, targets, usable, columns)
    dquant = lax.dot_general(dlogits, hidden, contract_tokens, preferred_element_type=jnp.float32)
    hidden_part = jnp.dot(dlogits, quantized, preferred_element_type=jnp.float32)
    scale_terms = jnp.sum(dquant * (levels - inside * ratios), axis=1)
    scale_sum = lax.psum(scale_terms, "width")
    grad_hidden = lax.psum(hidden_part, "vocab")
    grad_weight = inside * dquant + DECAY * usable.astype(jnp.float32)[:, None] * weight
    grad_scale = scale_sum * (1.0 / math.sqrt(D * 7.0))
    return (grad_weight, grad_scale, grad_hidden, loss)


def solution(mesh):
    placed = (P(None, "width"), P("vocab", "width"), P("vocab"), P("vocab"), P())
    return jax.shard_map(
        per_device,
        mesh=mesh,
        in_specs=placed,
        out_specs=(P("vocab", "width"), P("vocab"), P(None, "width"), P()),
        check_vma=False,
    )
```

profile of v0, /device:TPU:1, one launch (start us, length us, event | category | flops | bytes accessed | tf_op | source)
XLA Modules:
  0.0 350.0 jit_solution(7827806842242293340)
XLA Ops:
  7.2 0.0 copy-start
  7.2 0.0 all-reduce.4.cloned.1.call-start
  7.2 1.0 copy-done
  8.3 4.2 %convolution_bitcast_fusion = f32[512,1024]{0,1:T(8,128)} fusion(bf16[512,672]{0,1:T(8,128)(2,1)S(1)} %copy-done, f32[1024]{0:T(1024)} %param.7, f32[1024,672]{0,1:T(8,128)} %param.6), kind=kOutput, calls=%fused_computation.13 | convolution fusion | flops 708771840 | bytes 5541888 | tf_op jit(solution)/shard_map/dot_general | solution.py:44
  12.4 0.0 copy-start.2
  12.4 0.0 copy-start.3
  12.4 0.0 all-reduce.4.cloned.1.call-update
  12.4 0.0 all-reduce.6.cloned.1.call-start
  12.5 0.6 copy-done.2
  13.1 82.2 %all-reduce.4.cloned.1.call-done = f32[512,1024]{0,1:T(8,128)} async-done(((f32[512,1024]{0,1:T(8,128)}), f32[512,1024]{0,1:T(8,128)}) %all-reduce.4.cloned.1.call-update) | async-done | bytes 2097168 | tf_op jit(solution)/shard_map/psum | solution.py:47
  95.3 0.0 copy-start.1
  95.3 0.0 copy-start.4
  95.3 2.0 select_reduce_fusion
  97.3 65.7 %pmax.7 = f32[512]{0:T(512)S(1)} all-reduce(f32[512]{0:T(512)S(1)} %select_reduce_fusion), channel_id=1, replica_groups=mesh['vocab'=32,'width'=8] {'vocab'}, use_global_device_ids=true, to_apply=%region_2.3 | all-reduce | flops 512 | bytes 4096 | tf_op jit(solution)/shard_map/pmax | solution.py:29
  163.0 0.0 copy-done.3
  163.0 0.0 copy-done.1
  163.0 0.9 fusion.2
  163.9 64.0 %all-reduce = (f32[512]{0:T(512)S(1)}, f32[512]{0:T(512)S(1)}) all-reduce(f32[512]{0:T(512)S(1)} %get-tuple-element.5, f32[512]{0:T(512)S(1)} %get-tuple-element.4), channel_id=1, replica_groups=mesh['vocab'=32,'width'=8] {'vocab'}, use_global_device_ids=true, to_apply=%region_4.5 | all-reduce | flops 1024 | bytes 8192 | tf_op jit(solution)/shard_map/psum | solution.py:31
  227.9 0.0 copy-done.4
  227.9 4.2 %fusion.4 = f32[512,672]{0,1:T(8,128)} fusion(f32[1024]{0:T(1024)S(1)} %copy-done.4, f32[1024,672]{0,1:T(8,128)} %param.6, f32[512,1024]{0,1:T(8,128)S(1)} %copy-done.1, s32[512]{0:T(512)S(1)} %copy-done.3, f32[512]{0:T(512)S(1)} %get-tuple-element.6, f32[512]{0:T(512)S(1)} %pmax.7, s32[1024]{0:T(1024)S(1)} %iota_add_fusion, ...), kind=kOutput, calls=%fused_computation.15 | convolution fusion | flops 712441856 | bytes 6241280 | tf_op jit(solution)/shard_map/dot_general | solution.py:50
  232.1 0.0 all-reduce.6.cloned.1.call-update
  232.1 5.0 %multiply_reduce_fusion = (f32[1024]{0:T(1024)S(1)}, f32[1024,672]{0,1:T(8,128)}) fusion(f32[1024,672]{0,1:T(8,128)} %param.6, f32[1024]{0:T(1024)S(1)} %copy-done.4, f32[1024]{0:T(1024)S(1)} %get-tuple-element.8, bf16[512,672]{0,1:T(8,128)(2,1)S(1)} %copy-done, f32[512,1024]{0,1:T(8,128)S(1)} %copy-done.1, s32[512]{0:T(512)S(1)} %copy-done.3, ...), kind=kOutput, calls=%fused_computation | convolution fusion | flops 717945856 | bytes 8313856 | tf_op jit(solution)/shard_map/dot_general | solution.py:49
  237.1 11.9 %psum.37 = f32[1024]{0:T(1024)S(1)} all-reduce(f32[1024]{0:T(1024)S(1)} %get-tuple-element.10), channel_id=1, replica_groups=mesh['vocab'=32,'width'=8] {'width'}, use_global_device_ids=true, to_apply=%region_6.7 | all-reduce | flops 1024 | bytes 8192 | tf_op jit(solution)/shard_map/psum | solution.py:52
  249.0 0.6 subtract_reduce_fusion
  249.6 0.6 broadcast_multiply_fusion
  250.2 90.4 %all-reduce.6.cloned.1.call-done = f32[512,672]{0,1:T(8,128)} async-done(((f32[512,672]{0,1:T(8,128)}), f32[512,672]{0,1:T(8,128)}) %all-reduce.6.cloned.1.call-update) | async-done | bytes 1376272 | tf_op jit(solution)/shard_map/psum | solution.py:53
  340.6 2.5 copy.11
  (2 shorter events, 0.0 us)
Async XLA Ops:
  7.2 1.1 copy-start
  7.2 88.1 %all-reduce.4.cloned.1.call-start = ((), (), s32[]{:S(2)}) async-start(), calls=%async_computation | async-start | bytes 4194304 | tf_op jit(solution)/shard_map/psum | solution.py:47
  12.4 0.7 copy-start.2
  12.4 150.5 %copy-start.3 = (s32[512]{0:T(512)S(1)}, s32[512]{0:T(512)}, u32[]{:S(2)}) copy-start(s32[512]{0:T(512)} %param.9) | copy-start | bytes 6148
  12.4 328.2 %all-reduce.6.cloned.1.call-start = ((), (), s32[]{:S(2)}) async-start(), calls=%async_computation.1 | async-start | bytes 2752512 | tf_op jit(solution)/shard_map/psum | solution.py:53
  95.3 67.7 %copy-start.1 = (f32[512,1024]{0,1:T(8,128)S(1)}, f32[512,1024]{0,1:T(8,128)}, u32[]{:S(2)}) copy-start(f32[512,1024]{0,1:T(8,128)} %all-reduce.4.cloned.1.call-done) | copy-start | bytes 6291460
  95.3 132.6 %copy-start.4 = (f32[1024]{0:T(1024)S(1)}, f32[1024]{0:T(1024)}, u32[]{:S(2)}) copy-start(f32[1024]{0:T(1024)} %param.7) | copy-start | bytes 12292
Sparse Core Ops, SparseCore 0:
  12.6 82.6 all-reduce.3
  232.2 108.3 all-reduce.5
where the time goes:
time: 350 us
  waiting for transfers between devices  173 us (49%)
  blocking collectives  142 us (41%)
  between operations  14.1 us (4%)
  matrix products  13.4 us (4%)
  local copies, waits for them, and re-layouts  4.17 us (1%)
  other arithmetic  4.12 us (1%)
    psum x1, waiting for transfers between devices, per_device(): grad_hidden = lax.psum(hidden_part, 'vocab')  90.4 us
    psum x1, waiting for transfers between devices, per_device(): logits = lax.psum(partial_value, 'width')  82.2 us
    pmax x1, blocking collectives, softmax_rows(): row_top = lax.pmax(local_top, 'vocab')  65.7 us
    psum x1, blocking collectives, softmax_rows(): row_total, picked = lax.psum((jnp.sum(exp_terms, axis=1), picked), 'vocab')  64 us
    psum x1, blocking collectives, per_device(): scale_sum = lax.psum(scale_terms, 'width')  11.9 us
  transfers between devices with their start and end apart: 2, of which 2 were waited for; matrix products, arithmetic and copies ran while one was open for 2% of the time, Pallas kernels for 0%

commit v1 on v0

v1 whole, which is shorter than its diff:
```python
import functools
import math

import jax
import jax.numpy as jnp
from jax import lax
from jax.experimental import pallas as pl
from jax.experimental.pallas import tpu as pltpu
from jax.sharding import PartitionSpec as P

D = 5376
NEG_FILL = -1e30
DECAY = 0.1
MESH = pl.DeviceIdType.MESH

NZ = 8
NG = 8
NY = 4
TB = 64
NS = 4
HB = TB // NS
ROWS = 1024
COLS = 672
PAD = 768
FOLD = 384

CODE_TOP = 32000.0
UNIT = math.log(2.0) / 256.0
ROOT_TOP = 65535.0
ROOT_MID = 32768.0


def code_step(x, top_code, axis):
    top = jnp.max(jnp.abs(x), axis=axis, keepdims=True)
    e = jnp.ceil(jnp.log(jnp.maximum(top, 1e-30) * (1.0 / top_code)) * (1.0 / UNIT))
    return e, jnp.exp(e * (-UNIT))


def to_codes(x, inv):
    return jnp.floor(x * inv + 0.5)


def kernel(
    hid_hbm, w_hbm, sc_hbm, fl_hbm, tg_hbm,
    gw_out, gs_out, gh_out, loss_out,
    w_v, sc1, fl1, tg4, ht_s, q_s, h_s, part, dl_s, tr_s, zt_s, own_s, root_s,
    rs_out, rs_in, ag_s, st_a, st_b, st_z, gh_s, a_out, a_in, b_buf, c_buf, f_buf,
    w_sem, h_sem, small_sem,
    rs_send, rs_recv, ag_send, ag_recv,
    sa_send, sa_recv, sb_send, sb_recv, sz_send, sz_recv,
    a_send, a_recv, b_send, b_recv, c_send, c_recv, f_send, f_recv,
):
    f32, bf16, i32, i16 = jnp.float32, jnp.bfloat16, jnp.int32, jnp.int16
    v = lax.axis_index("vocab")
    w = lax.axis_index("width")
    core = lax.rem(v, 2)
    x = lax.rem(lax.div(v, 2), 4)
    y = lax.div(v, 8)
    right = (v, lax.rem(w + 1, NZ))
    left = (v, lax.rem(w + NZ - 1, NZ))

    def g_index(mode):
        return (x if mode == "x" else y) * 2 + core

    def g_peer(mode, j):
        other = lax.rem(g_index(mode) + j, NG)
        far, far_core = lax.div(other, 2), lax.rem(other, 2)
        if mode == "x":
            return other, ((y * 4 + far) * 2 + far_core, w)
        return other, ((far * 4 + x) * 2 + far_core, w)

    def y_index(mode):
        return y if mode == "x" else x

    def y_peer(mode, j):
        other = lax.rem(y_index(mode) + j, NY)
        if mode == "x":
            return other, ((other * 4 + x) * 2 + core, w)
        return other, ((y * 4 + other) * 2 + core, w)

    def z_peer(j):
        return (v, lax.rem(w + j, NZ))

    def block_rows(shift, half=None):
        block = lax.rem(w + (shift + 2 * NZ), NZ)
        if half is None:
            return pl.ds(pl.multiple_of(block * TB, TB), TB)
        return pl.ds(pl.multiple_of(block * TB + half * HB, HB), HB)

    small_copies = [
        pltpu.make_async_copy(src, dst, small_sem.at[i])
        for i, (src, dst) in enumerate([(tg_hbm, tg4), (sc_hbm, sc1), (fl_hbm, fl1)])
    ]
    for copy in small_copies:
        copy.start()
    WB = 256

    def w_copy(i):
        cols = pl.ds(pl.multiple_of(i * WB, WB), WB)
        return pltpu.make_async_copy(w_hbm.at[:, cols], w_v.at[:, cols], w_sem.at[i])

    @pl.loop(0, ROWS // WB)
    def _(i):
        w_copy(i).start()

    h_copy = pltpu.make_async_copy(hid_hbm, ht_s.at[pl.ds(0, COLS)], h_sem)
    h_copy.start()

    barrier = pltpu.get_barrier_semaphore()
    for j in range(1, NZ):
        pl.semaphore_signal(barrier, inc=1, device_id=z_peer(j), device_id_type=MESH)
    for j in range(1, NG):
        pl.semaphore_signal(
            barrier, inc=1, device_id=g_peer("x", j)[1], device_id_type=MESH
        )
    for j in range(2, NG):
        far = lax.rem(y + lax.div(j, 2), 4)
        pl.semaphore_signal(
            barrier,
            inc=1,
            device_id=((far * 4 + x) * 2 + j % 2, w),
            device_id_type=MESH,
        )

    for copy in small_copies:
        copy.wait()
    tr_s[...] = jnp.transpose(
        jnp.concatenate([tg4[...].astype(f32), jnp.zeros((124, 128), f32)], axis=0)
    )
    ht_s[COLS:, :] = jnp.zeros((PAD - COLS, 512), bf16)
    q_s[COLS:, :] = jnp.zeros((PAD - COLS, ROWS), bf16)
    h_copy.wait()

    @pl.loop(0, ROWS // WB)
    def _(i):
        w_copy(i).wait()
        tokens = pl.ds(pl.multiple_of(i * 128, 128), 128)
        h_s[tokens, :] = jnp.transpose(ht_s[:, tokens])
        cols = pl.ds(pl.multiple_of(i * WB, WB), WB)
        scale = sc1[:, cols]
        rounded = jnp.floor(w_v[:, cols] * (1.0 / scale) + 0.5)
        levels = jnp.clip(rounded, -8.0, 7.0)
        q_s[:COLS, cols] = (scale * levels).astype(bf16)

    def logits_of(shifts):
        rows = [h_s[block_rows(shift), :] for shift in shifts]
        values = jnp.dot(
            jnp.concatenate(rows, axis=0) if len(shifts) > 1 else rows[0],
            q_s[...],
            preferred_element_type=f32,
        )
        for i, shift in enumerate(shifts):
            part[block_rows(shift), :] = values[i * TB : (i + 1) * TB, :]

    logits_of((4,))
    pl.semaphore_wait(barrier, (NZ - 1) + (NG - 1) + (NG - 2))

    lane_half = lax.broadcasted_iota(i32, (HB, 128), 1)

    def rs_copy(way, step, half):
        return pltpu.make_async_remote_copy(
            src_ref=rs_out.at[way, step, half],
            dst_ref=rs_in.at[way, step, half],
            send_sem=rs_send.at[way, step, half],
            recv_sem=rs_recv.at[way, step, half],
            device_id=right if way == 0 else left,
            device_id_type=MESH,
        )

    def encode(value, ref):
        e, inv = code_step(value, 4.0 * CODE_TOP, 1)
        codes = to_codes(value, inv).astype(i32)
        ref[:, :ROWS] = (codes >> 2).astype(i16)
        low = codes & 3
        pairs = low[:, :128]
        for i in range(1, ROWS // 128):
            pairs = pairs | (low[:, i * 128 : (i + 1) * 128] << (2 * i))
        ref[:, ROWS:] = jnp.where(lane_half == 0, e.astype(i32), pairs).astype(i16)

    def decode(ref):
        high = ref[:, :ROWS].astype(i32) << 2
        pairs = ref[:, ROWS:].astype(i32)
        unit = jnp.exp(pairs[:, :1].astype(f32) * UNIT)
        blocks = []
        for i in range(ROWS // 128):
            low = jnp.where(lane_half == 0, 1.5, ((pairs >> (2 * i)) & 3).astype(f32))
            blocks.append(high[:, i * 128 : (i + 1) * 128].astype(f32) + low)
        return jnp.concatenate(blocks, axis=1) * unit

    def rs_get(way, step, sub):
        return decode(rs_in.at[way, step, sub])

    def mine(shift, half):
        return part[block_rows(shift, half), :]

    firsts = ([s for s in range(NS) if s < NS // 2], [s for s in range(NS) if s >= NS // 2])

    def rs_pair(n, add):
        step = lax.div(n, NS)
        subs = (lax.rem(n + NS // 2, NS), lax.rem(n, NS))
        if add:
            for way in (0, 1):
                rs_copy(way, step - 1, subs[way]).wait_recv()
        values = [mine(4 - step, subs[0]), mine(step - 4, subs[1])]
        if add:
            values = [values[way] + rs_get(way, step - 1, subs[way]) for way in (0, 1)]
        for way in (0, 1):
            encode(values[way], rs_out.at[way, step, subs[way]])
        for way in (0, 1):
            rs_copy(way, step, subs[way]).start()

    @pl.loop(NS // 2, NS)
    def _(n):
        rs_pair(n, False)

    logits_of((3, -3))

    @pl.loop(NS, NS + NS // 2)
    def _(n):
        rs_pair(n, False)

    logits_of((2, -2))

    @pl.loop(NS + NS // 2, 2 * NS)
    def _(n):
        rs_pair(n, True)

    logits_of((1, -1, 0))

    @pl.loop(2 * NS, 4 * NS)
    def _(n):
        rs_pair(n, True)

    def ag_ref(way, step, sub):
        block = lax.rem(w + (step if way == 1 else NZ - step), NZ)
        return ag_s.at[block, sub]

    def ag_copy(way, step, sub):
        ref = ag_ref(way, step, sub)
        return pltpu.make_async_remote_copy(
            src_ref=ref,
            dst_ref=ref,
            send_sem=ag_send.at[way, step, sub],
            recv_sem=ag_recv.at[way, step, sub],
            device_id=right if way == 0 else left,
            device_id_type=MESH,
        )

    def ag_wait(way, step, sub):
        ref = ag_ref(way, step + 1, sub)
        pltpu.make_async_copy(ref, ref, ag_recv.at[way, step, sub]).wait()

    def ag_step(step):
        for sub in range(NS):
            for way in (0, 1):
                ag_wait(way, step, sub)
                if sub in firsts[way]:
                    ag_copy(way, step + 1, sub).start()
                else:

                    @pl.when(step < 2)
                    def _():
                        ag_copy(way, step + 1, sub).start()

    def ag_last():
        for way in (0, 1):
            for sub in firsts[way]:
                ag_wait(way, 3, sub)

    usable_row = fl1[...] == 0

    def pick_lane(ref, index, rows):
        at = lax.broadcasted_iota(i32, (rows.size, 128), 1)
        return jnp.sum(jnp.where(at == index, ref[rows, :], 0.0), axis=1, keepdims=True)

    def hits(block, first, count):
        rows = pl.ds(pl.multiple_of(lax.rem(block, 2) * TB + first, count), count)
        column = pick_lane(tr_s, lax.div(block, 2), rows).astype(i32) - v * ROWS
        return lax.broadcasted_iota(i32, (count, ROWS), 1) == column

    @pl.loop(0, NS)
    def _(sub):
        for way in (0, 1):
            rs_copy(way, 3, sub).wait_recv()
        own = mine(0, sub) + rs_get(0, 3, sub) + rs_get(1, 3, sub)
        masked = jnp.where(usable_row, own, NEG_FILL)
        top = jnp.max(masked, axis=1, keepdims=True)
        root = jnp.where(usable_row, jnp.exp((masked - top) * 0.5), 0.0)
        codes = jnp.floor(root * ROOT_TOP + (0.5 - ROOT_MID))
        ag_s[w, sub] = codes.astype(i32).astype(i16)
        for way in (0, 1):
            ag_copy(way, 0, sub).start()
        rows = pl.ds(pl.multiple_of(sub * HB, HB), HB)
        part[block_rows(0, sub), :] = own
        root_s[rows, :] = root
        own_s[rows, :] = jnp.broadcast_to(top, (HB, 128))

    lane = lax.broadcasted_iota(i32, (TB, 128), 1)
    total = jnp.sum(root_s[...] * root_s[...], axis=1, keepdims=True)
    picked = jnp.sum(
        jnp.where(hits(w, 0, TB), part[block_rows(0), :], 0.0), axis=1, keepdims=True
    )
    stats = jnp.where(
        lane == 0,
        own_s[...],
        jnp.where(lane == 1, total, jnp.where(lane == 2, picked, 0.0)),
    )

    stats = jnp.transpose(jnp.concatenate([stats, jnp.zeros((TB, 128), f32)], axis=0))
    g = g_index("x")
    st_a[g] = stats[:8, :]
    for j in range(1, NG):
        pltpu.make_async_remote_copy(
            src_ref=st_a.at[g], dst_ref=st_a.at[g], send_sem=sa_send, recv_sem=sa_recv,
            device_id=g_peer("x", j)[1], device_id_type=MESH,
        ).start()

    def wait_bytes(ref, sem):
        pltpu.make_async_copy(ref, ref, sem).wait()

    def merge(buf, n):
        best = buf[0, 0:1, :]
        for i in range(1, n):
            best = jnp.maximum(best, buf[i, 0:1, :])
        weight = jnp.zeros((1, 128), f32)
        pick = jnp.zeros((1, 128), f32)
        for i in range(n):
            weight += buf[i, 1:2, :] * jnp.exp(buf[i, 0:1, :] - best)
            pick += buf[i, 2:3, :]
        return best, weight, pick

    @pl.loop(0, 3)
    def _(step):
        ag_step(step)

        @pl.when(step == 0)
        def _():
            wait_bytes(st_a.at[pl.ds(0, NG - 1)], sa_recv)
            best, weight, pick = merge(st_a, NG)
            st_b[y] = jnp.concatenate([best, weight, pick, jnp.zeros((5, 128), f32)], axis=0)
            for j in range(1, NY):
                pltpu.make_async_remote_copy(
                    src_ref=st_b.at[y], dst_ref=st_b.at[y], send_sem=sb_send, recv_sem=sb_recv,
                    device_id=y_peer("x", j)[1], device_id_type=MESH,
                ).start()

        @pl.when(step == 1)
        def _():
            wait_bytes(st_b.at[pl.ds(0, NY - 1)], sb_recv)
            best, weight, pick = merge(st_b, NY)
            lane_row = lax.broadcasted_iota(i32, (1, 128), 1)
            loss_row = jnp.where(lane_row < TB, best + jnp.log(weight) - pick, 0.0)
            f_buf[w, pl.ds(8, 8), :] = jnp.broadcast_to(loss_row, (8, 128))
            factor = jnp.exp(st_a[g, 0:1, :] - best) / weight
            st_z[w] = jnp.broadcast_to(factor * (1.0 / (ROOT_TOP * ROOT_TOP)), (8, 128))
            for j in range(1, NZ):
                pltpu.make_async_remote_copy(
                    src_ref=st_z.at[w], dst_ref=st_z.at[w], send_sem=sz_send, recv_sem=sz_recv,
                    device_id=z_peer(j), device_id_type=MESH,
                ).start()

    wait_bytes(st_z.at[pl.ds(0, NZ - 1)], sz_recv)
    rows_of = [st_z[i, 0:1, :] for i in range(NZ)]
    zt_s[...] = jnp.transpose(
        jnp.concatenate(rows_of + [jnp.zeros((120, 128), f32)], axis=0)
    )

    def form_dlogits(shift):
        block = lax.rem(w + (shift + NZ), NZ)
        factor = pick_lane(zt_s, block, pl.ds(0, TB))
        codes = jnp.concatenate([ag_s[block, s] for s in range(NS)], axis=0)
        root = codes.astype(i32).astype(f32) + ROOT_MID
        dl_s[block_rows(shift), :] = (
            root * root * factor - hits(block, 0, TB).astype(f32)
        ).astype(bf16)

    groups = [(-1, 0, 1), (-2, 2), (-3, 3), (4,)]
    modes = ["x", "y", "y", "x"]
    nt = (((1,), (1,)), ((), ()))

    def fold(x):
        n = x.shape[0] // 8
        e, inv = code_step(x, CODE_TOP, 1)
        wide = lax.broadcasted_iota(i32, (8 * n, PAD), 1)
        codes = jnp.where(wide < COLS, to_codes(x, inv), e).astype(i32)
        return jnp.concatenate(
            [codes[:, :FOLD].reshape(n, 8, FOLD), codes[:, FOLD:].reshape(n, 8, FOLD)], axis=1
        ).astype(i16)

    def unfold(piece):
        n = piece.shape[0]
        codes = piece.astype(i32).astype(f32)
        low = codes[:, :8, :].reshape(8 * n, FOLD)
        high = codes[:, 8:, :].reshape(8 * n, FOLD)
        unit = jnp.exp(high[:, FOLD - 1 :] * UNIT)
        wide = jnp.concatenate([low, high], axis=1)
        lane_pad = lax.broadcasted_iota(i32, (8 * n, PAD), 1)
        return jnp.where(lane_pad < COLS, wide * unit, 0.0)

    def stage_a(k):
        n = len(groups[k])
        terms = [dl_s[block_rows(shift), :] for shift in groups[k]]
        term = lax.dot_general(
            jnp.concatenate(terms, axis=0) if n > 1 else terms[0],
            q_s[...],
            nt,
            preferred_element_type=f32,
        )
        g = g_index(modes[k])
        for s in range(n):
            a_out[k, :, s] = fold(term[s * TB : (s + 1) * TB])
        a_in[k, g] = a_out[k, g]
        for j in range(1, NG):
            other, device = g_peer(modes[k], j)
            pltpu.make_async_remote_copy(
                src_ref=a_out.at[k, other, pl.ds(0, n)], dst_ref=a_in.at[k, g, pl.ds(0, n)],
                send_sem=a_send.at[k], recv_sem=a_recv.at[k],
                device_id=device, device_id_type=MESH,
            ).start()

    def stage_b(k):
        n = len(groups[k])
        wait_bytes(a_in.at[k, pl.ds(0, NG - 1), pl.ds(0, n)], a_recv.at[k])
        total = unfold(a_in[k, 0, :n])
        for i in range(1, NG):
            total += unfold(a_in[k, i, :n])
        at = y_index(modes[k])
        b_buf[k, at, :n] = fold(total)
        for j in range(1, NY):
            mine_ref = b_buf.at[k, at, pl.ds(0, n)]
            pltpu.make_async_remote_copy(
                src_ref=mine_ref, dst_ref=mine_ref,
                send_sem=b_send.at[k], recv_sem=b_recv.at[k],
                device_id=y_peer(modes[k], j)[1], device_id_type=MESH,
            ).start()

    def stage_c(k):
        n = len(groups[k])
        wait_bytes(b_buf.at[k, pl.ds(0, NY - 1), pl.ds(0, n)], b_recv.at[k])
        total = unfold(b_buf[k, 0, :n])
        for i in range(1, NY):
            total += unfold(b_buf[k, i, :n])
        g = g_index(modes[k])
        c_buf[k, g, :n] = fold(total)
        for j in range(1, NG):
            mine_ref = c_buf.at[k, g, pl.ds(0, n)]
            pltpu.make_async_remote_copy(
                src_ref=mine_ref, dst_ref=mine_ref,
                send_sem=c_send.at[k], recv_sem=c_recv.at[k],
                device_id=g_peer(modes[k], j)[1], device_id_type=MESH,
            ).start()

    odd = lax.rem(w, 2)
    unit_blocks = [w, w + 2 * odd - 1, w + 2 - 4 * odd, w + 4]

    def unit_lanes(k):
        unit = lax.div(lax.rem(unit_blocks[k] + NZ, NZ), 2)
        return pl.ds(pl.multiple_of(unit * 128, 128), 128)

    def stage_d(k):
        n = len(groups[k])
        wait_bytes(c_buf.at[k, pl.ds(0, NG - 1), pl.ds(0, n)], c_recv.at[k])
        for s, shift in enumerate(groups[k]):
            gh_s[block_rows(shift), :] = unfold(c_buf[k, :, s])
        gh_out[:, unit_lanes(k)] = jnp.transpose(gh_s[unit_lanes(k), :])[:COLS, :]

    GB = 256

    def rows_grad(b):
        cols = pl.ds(pl.multiple_of(b * GB, GB), GB)
        dquant = jnp.dot(ht_s[:COLS, :], dl_s[:, cols], preferred_element_type=f32)
        usable = (fl1[:, cols] == 0).astype(f32)
        ratios = w_v[:, cols] * (1.0 / sc1[:, cols])
        rounded = jnp.floor(ratios + 0.5)
        levels = jnp.clip(rounded, -8.0, 7.0)
        inside = (rounded == levels).astype(f32)
        gw_out[:, cols] = inside * dquant + (DECAY * usable) * w_v[:, cols]
        terms = jnp.sum(dquant * (levels - inside * ratios), axis=0, keepdims=True)
        for i in range(GB // 128):
            f_buf[w, pl.ds(b * (GB // 128) + i, 1), :] = terms[:, i * 128 : (i + 1) * 128]

    @pl.loop(0, 7)
    def _(i):
        form_dlogits(i - 3)

    stage_a(0)
    stage_a(1)
    stage_a(2)
    ag_last()
    form_dlogits(4)
    stage_a(3)

    @pl.loop(0, 2)
    def _(b):
        rows_grad(b)

    stage_b(0)
    stage_b(1)
    stage_b(2)
    stage_b(3)

    @pl.loop(2, 4)
    def _(b):
        rows_grad(b)

    for j in range(1, NZ):
        pltpu.make_async_remote_copy(
            src_ref=f_buf.at[w], dst_ref=f_buf.at[w], send_sem=f_send, recv_sem=f_recv,
            device_id=z_peer(j), device_id_type=MESH,
        ).start()
    stage_c(0)
    stage_c(1)
    stage_c(2)
    stage_c(3)
    wait_bytes(f_buf.at[pl.ds(0, NZ - 1)], f_recv)
    tail = f_buf[0]
    for i in range(1, NZ):
        tail += f_buf[i]
    gs_out[...] = tail[:8, :] * (1.0 / math.sqrt(D * 7.0))
    loss_out[...] = jnp.sum(tail[8:9, :], axis=1, keepdims=True)
    stage_d(0)
    stage_d(1)
    stage_d(2)
    stage_d(3)

    for k in range(len(groups)):
        n = len(groups[k])
        wait_bytes(a_out.at[k, pl.ds(0, NG - 1), pl.ds(0, n)], a_send.at[k])
        wait_bytes(b_buf.at[k, pl.ds(0, NY - 1), pl.ds(0, n)], b_send.at[k])
        wait_bytes(c_buf.at[k, pl.ds(0, NG - 1), pl.ds(0, n)], c_send.at[k])
    wait_bytes(st_a.at[pl.ds(0, NG - 1)], sa_send)
    wait_bytes(st_b.at[pl.ds(0, NY - 1)], sb_send)
    wait_bytes(st_z.at[pl.ds(0, NZ - 1)], sz_send)
    wait_bytes(f_buf.at[pl.ds(0, NZ - 1)], f_send)
    for way in (0, 1):
        for step in range(4):
            for sub in range(NS):
                if step > 0 or sub in firsts[way]:
                    rs_copy(way, step, sub).wait_send()
                if step < 3 or sub in firsts[way]:
                    ag_copy(way, step, sub).wait_send()


def per_device(hidden, weight, scale, flags, targets):
    f32, bf16, i16 = jnp.float32, jnp.bfloat16, jnp.int16
    vmem = pl.BlockSpec(memory_space=pltpu.VMEM)
    anywhere = pl.BlockSpec(memory_space=pl.ANY)
    dma = pltpu.SemaphoreType.DMA
    grad_weight, grad_scale, grad_hidden, loss = pl.pallas_call(
        kernel,
        out_shape=(
            pltpu.VMEM((COLS, ROWS), f32),
            jax.ShapeDtypeStruct((8, 128), f32),
            pltpu.VMEM((COLS, 512), f32),
            jax.ShapeDtypeStruct((1, 1), f32),
        ),
        in_specs=[anywhere] * 5,
        out_specs=(vmem, vmem, vmem, vmem),
        scratch_shapes=[
            pltpu.VMEM((COLS, ROWS), f32),
            pltpu.VMEM((1, ROWS), f32),
            pltpu.VMEM((1, ROWS), jnp.int32),
            pltpu.VMEM((4, 128), jnp.int32),
            pltpu.VMEM((PAD, 512), bf16),
            pltpu.VMEM((PAD, ROWS), bf16),
            pltpu.VMEM((512, PAD), bf16),
            pltpu.VMEM((512, ROWS), f32),
            pltpu.VMEM((512, ROWS), bf16),
            pltpu.VMEM((128, 128), f32),
            pltpu.VMEM((128, 128), f32),
            pltpu.VMEM((TB, 128), f32),
            pltpu.VMEM((TB, ROWS), f32),
            pltpu.VMEM((2, 4, NS, HB, ROWS + 128), i16),
            pltpu.VMEM((2, 4, NS, HB, ROWS + 128), i16),
            pltpu.VMEM((NZ, NS, HB, ROWS), i16),
            pltpu.VMEM((NG, 8, 128), f32),
            pltpu.VMEM((NY, 8, 128), f32),
            pltpu.VMEM((NZ, 8, 128), f32),
            pltpu.VMEM((512, PAD), f32),
            pltpu.VMEM((4, NG, 3, 16, FOLD), i16),
            pltpu.VMEM((4, NG, 3, 16, FOLD), i16),
            pltpu.VMEM((4, NY, 3, 16, FOLD), i16),
            pltpu.VMEM((4, NG, 3, 16, FOLD), i16),
            pltpu.VMEM((NZ, 16, 128), f32),
            dma((4,)),
            dma(()),
            dma((3,)),
            dma((2, 4, NS)),
            dma((2, 4, NS)),
            dma((2, 4, NS)),
            dma((2, 4, NS)),
            dma(()),
            dma(()),
            dma(()),
            dma(()),
            dma(()),
            dma(()),
            dma((4,)),
            dma((4,)),
            dma((4,)),
            dma((4,)),
            dma((4,)),
            dma((4,)),
            dma(()),
            dma(()),
        ],
        compiler_params=pltpu.CompilerParams(
            collective_id=0, has_side_effects=True, vmem_limit_bytes=58 * 1024 * 1024
        ),
    )(
        hidden.T,
        weight.T,
        scale.reshape(1, ROWS),
        flags.reshape(1, ROWS),
        targets.reshape(4, 128),
    )
    return (grad_weight.T, grad_scale.reshape(ROWS), grad_hidden.T, loss.reshape(()))


def solution(mesh):
    placed = (P(None, "width"), P("vocab", "width"), P("vocab"), P("vocab"), P())
    return jax.shard_map(
        per_device,
        mesh=mesh,
        in_specs=placed,
        out_specs=(P("vocab", "width"), P("vocab"), P(None, "width"), P()),
        check_vma=False,
    )
```

time: 350 us -> 68 us (0.19)
  waiting for transfers between devices: 173 us -> 0 us
  blocking collectives: 142 us -> 0 us
  Pallas kernels: 0 us -> 62.2 us
  matrix products: 13.4 us -> 0 us
  between operations: 14.1 us -> 2.4 us
  other arithmetic: 4.12 us -> 0 us
    psum x2 -> x0, waiting for transfers between devices: 173 us -> none  [the longest x1 90.4 us: per_device(): grad_hidden = lax.psum(hidden_part, 'vocab')]
    psum x2 -> x0, blocking collectives: 75.8 us -> none  [the longest x1 64 us: softmax_rows(): row_total, picked = lax.psum((jnp.sum(exp_terms, axis=1), picked), 'vocab')]
    pmax x1 -> x0, blocking collectives: 65.7 us -> none  [softmax_rows(): row_top = lax.pmax(local_top, 'vocab')]
    pallas_call x0 -> x1, Pallas kernels: none -> 62.2 us  [per_device(): pl.pallas_call(kernel, out_shape=(pltpu.VMEM((COLS, ROWS), f32), jax.Shap...]
    dot_general x3 -> x0, matrix products: 13.4 us -> none  [the longest x1 5.02 us: per_device(): lax.dot_general(dlogits, hidden, contract_tokens, preferred_element_type=...]
  transfers between devices with their start and end apart: 2 -> 0, of which waited for: 2 -> 0; matrix products, arithmetic and copies ran while one was open for 2% -> 0% of each run, Pallas kernels for 0% -> 0%
where the time goes in v1:
time: 68 us; the launch traced here: 67.8 us
  Pallas kernels  62.2 us (91%)
  local copies, waits for them, and re-layouts  3.21 us (5%)
  between operations  2.4 us (4%)
    pallas_call x1, Pallas kernels, per_device(): pl.pallas_call(kernel, out_shape=(pltpu.VMEM((COLS, ROWS), f32), jax.Shap...  62.2 us
    unnamed x5, local copies, waits for them, and re-layouts  3.21 us

profile of v1, /device:TPU:1, one launch (start us, length us, event | category | flops | bytes accessed | tf_op | source)
XLA Modules:
  0.0 67.8 jit_solution(3025642385967619099)
XLA Ops:
  0.6 62.2 %shard_map.84 = (f32[672,1024]{1,0:T(8,128)S(1)}, f32[8,128]{1,0:T(8,128)}, f32[672,512]{1,0:T(8,128)S(1)}, f32[1,1]{1,0:T(1,128)}) custom-call(bf16[672,512]{1,0:T(8,128)(2,1)} %bitcast.12, f32[672,1024]{1,0:T(8,128)} %bitcast.11, f32[1,1024]{1,0:T(1,128)} %bitcast.13, s32[1,1024]{1,0:T(1,128)} %bitcast.14, s32[4,128]{1,0:T(4,128)} %bitcast.16), custom_call_target="tpu_custom_call" | custom-call | tf_op jit(solution)/shard_map/pallas_call | solution.py:549
  62.9 1.5 %copy.13 = f32[1024,672]{0,1:T(8,128)} copy(f32[1024,672]{0,1:T(8,128)S(1)} %bitcast.9) | data formatting | bytes 5505024
  64.4 0.0 copy-start
  64.4 1.1 %copy.14 = f32[512,672]{0,1:T(8,128)} copy(f32[512,672]{0,1:T(8,128)S(1)} %bitcast.10) | data formatting | bytes 2752512
  65.5 0.0 copy-done
  65.5 0.6 copy.15
Async XLA Ops:
  64.4 1.1 %copy-start = (f32[8,128]{1,0:T(8,128)S(1)}, f32[8,128]{1,0:T(8,128)}, u32[]{:S(2)}) copy-start(f32[8,128]{1,0:T(8,128)} %get-tuple-element.9) | copy-start | bytes 12292

commit v2 on v1

--- a/solution.py
+++ b/solution.py
@@ -329,53 +329,21 @@
             pick += buf[i, 2:3, :]
         return best, weight, pick
 
-    @pl.loop(0, 3)
-    def _(step):
-        ag_step(step)
-
-        @pl.when(step == 0)
-        def _():
-            wait_bytes(st_a.at[pl.ds(0, NG - 1)], sa_recv)
-            best, weight, pick = merge(st_a, NG)
-            st_b[y] = jnp.concatenate([best, weight, pick, jnp.zeros((5, 128), f32)], axis=0)
-            for j in range(1, NY):
-                pltpu.make_async_remote_copy(
-                    src_ref=st_b.at[y], dst_ref=st_b.at[y], send_sem=sb_send, recv_sem=sb_recv,
-                    device_id=y_peer("x", j)[1], device_id_type=MESH,
-                ).start()
-
-        @pl.when(step == 1)
-        def _():
-            wait_bytes(st_b.at[pl.ds(0, NY - 1)], sb_recv)
-            best, weight, pick = merge(st_b, NY)
-            lane_row = lax.broadcasted_iota(i32, (1, 128), 1)
-            loss_row = jnp.where(lane_row < TB, best + jnp.log(weight) - pick, 0.0)
-            f_buf[w, pl.ds(8, 8), :] = jnp.broadcast_to(loss_row, (8, 128))
-            factor = jnp.exp(st_a[g, 0:1, :] - best) / weight
-            st_z[w] = jnp.broadcast_to(factor * (1.0 / (ROOT_TOP * ROOT_TOP)), (8, 128))
-            for j in range(1, NZ):
-                pltpu.make_async_remote_copy(
-                    src_ref=st_z.at[w], dst_ref=st_z.at[w], send_sem=sz_send, recv_sem=sz_recv,
-                    device_id=z_peer(j), device_id_type=MESH,
-                ).start()
-
-    wait_bytes(st_z.at[pl.ds(0, NZ - 1)], sz_recv)
-    rows_of = [st_z[i, 0:1, :] for i in range(NZ)]
-    zt_s[...] = jnp.transpose(
-        jnp.concatenate(rows_of + [jnp.zeros((120, 128), f32)], axis=0)
-    )
-
     def form_dlogits(shift):
         block = lax.rem(w + (shift + NZ), NZ)
         factor = pick_lane(zt_s, block, pl.ds(0, TB))
+        dl_s[block_rows(shift), :] = (
+            part[block_rows(shift), :] * factor - hits(block, 0, TB).astype(f32)
+        ).astype(bf16)
+
+    def form_squares(shift):
+        block = lax.rem(w + (shift + NZ), NZ)
         codes = jnp.concatenate([ag_s[block, s] for s in range(NS)], axis=0)
         root = codes.astype(i32).astype(f32) + ROOT_MID
-        dl_s[block_rows(shift), :] = (
-            root * root * factor - hits(block, 0, TB).astype(f32)
-        ).astype(bf16)
-
-    groups = [(-1, 0, 1), (-2, 2), (-3, 3), (4,)]
-    modes = ["x", "y", "y", "x"]
+        part[block_rows(shift), :] = root * root
+
+    groups = [(0,), (-1, 1), (-2, 2), (-3, 3), (4,)]
+    modes = ["x", "x", "y", "y", "x"]
     nt = (((1,), (1,)), ((), ()))
 
     def fold(x):
@@ -399,6 +367,8 @@
 
     def stage_a(k):
         n = len(groups[k])
+        for shift in groups[k]:
+            form_dlogits(shift)
         terms = [dl_s[block_rows(shift), :] for shift in groups[k]]
         term = lax.dot_general(
             jnp.concatenate(terms, axis=0) if n > 1 else terms[0],
@@ -462,7 +432,9 @@
         wait_bytes(c_buf.at[k, pl.ds(0, NG - 1), pl.ds(0, n)], c_recv.at[k])
         for s, shift in enumerate(groups[k]):
             gh_s[block_rows(shift), :] = unfold(c_buf[k, :, s])
-        gh_out[:, unit_lanes(k)] = jnp.transpose(gh_s[unit_lanes(k), :])[:COLS, :]
+        if k > 0:
+            pair = unit_lanes(k - 1)
+            gh_out[:, pair] = jnp.transpose(gh_s[pair, :])[:COLS, :]
 
     GB = 256
 
@@ -479,16 +451,56 @@
         for i in range(GB // 128):
             f_buf[w, pl.ds(b * (GB // 128) + i, 1), :] = terms[:, i * 128 : (i + 1) * 128]
 
-    @pl.loop(0, 7)
-    def _(i):
-        form_dlogits(i - 3)
-
-    stage_a(0)
+    @pl.loop(0, 3)
+    def _(step):
+        ag_step(step)
+
+        @pl.loop(0, 2)
+        def _(side):
+            form_squares((step + 1) * (2 * side - 1))
+
+        @pl.when(step == 0)
+        def _():
+            wait_bytes(st_a.at[pl.ds(0, NG - 1)], sa_recv)
+            best, weight, pick = merge(st_a, NG)
+            st_b[y] = jnp.concatenate([best, weight, pick, jnp.zeros((5, 128), f32)], axis=0)
+            for j in range(1, NY):
+                pltpu.make_async_remote_copy(
+                    src_ref=st_b.at[y], dst_ref=st_b.at[y], send_sem=sb_send, recv_sem=sb_recv,
+                    device_id=y_peer("x", j)[1], device_id_type=MESH,
+                ).start()
+
+        @pl.when(step == 1)
+        def _():
+            wait_bytes(st_b.at[pl.ds(0, NY - 1)], sb_recv)
+            best, weight, pick = merge(st_b, NY)
+            lane_row = lax.broadcasted_iota(i32, (1, 128), 1)
+            loss_row = jnp.where(lane_row < TB, best + jnp.log(weight) - pick, 0.0)
+            f_buf[w, pl.ds(8, 8), :] = jnp.broadcast_to(loss_row, (8, 128))
+            factor = jnp.exp(st_a[g, 0:1, :] - best) / weight
+            factor = factor * (1.0 / (ROOT_TOP * ROOT_TOP))
+            st_z[w] = jnp.broadcast_to(factor, (8, 128))
+            for j in range(1, NZ):
+                pltpu.make_async_remote_copy(
+                    src_ref=st_z.at[w], dst_ref=st_z.at[w], send_sem=sz_send, recv_sem=sz_recv,
+                    device_id=z_peer(j), device_id_type=MESH,
+                ).start()
+            zt_s[...] = jnp.transpose(jnp.broadcast_to(factor, (128, 128)))
+            form_squares(0)
+            stage_a(0)
+
+    wait_bytes(st_z.at[pl.ds(0, NZ - 1)], sz_recv)
+    rows_of = [st_z[i, 0:1, :] for i in range(NZ)]
+    zt_s[...] = jnp.transpose(
+        jnp.concatenate(rows_of + [jnp.zeros((120, 128), f32)], axis=0)
+    )
+
     stage_a(1)
     stage_a(2)
+    stage_a(3)
     ag_last()
-    form_dlogits(4)
-    stage_a(3)
+    form_squares(4)
+    stage_a(4)
 
     @pl.loop(0, 2)
     def _(b):
@@ -498,6 +510,7 @@
     stage_b(1)
     stage_b(2)
     stage_b(3)
+    stage_b(4)
 
     @pl.loop(2, 4)
     def _(b):
@@ -512,6 +525,7 @@
     stage_c(1)
     stage_c(2)
     stage_c(3)
+    stage_c(4)
     wait_bytes(f_buf.at[pl.ds(0, NZ - 1)], f_recv)
     tail = f_buf[0]
     for i in range(1, NZ):
@@ -522,6 +536,7 @@
     stage_d(1)
     stage_d(2)
     stage_d(3)
+    stage_d(4)
 
     for k in range(len(groups)):
         n = len(groups[k])
@@ -577,10 +592,10 @@
             pltpu.VMEM((NY, 8, 128), f32),
             pltpu.VMEM((NZ, 8, 128), f32),
             pltpu.VMEM((512, PAD), f32),
-            pltpu.VMEM((4, NG, 3, 16, FOLD), i16),
-            pltpu.VMEM((4, NG, 3, 16, FOLD), i16),
-            pltpu.VMEM((4, NY, 3, 16, FOLD), i16),
-            pltpu.VMEM((4, NG, 3, 16, FOLD), i16),
+            pltpu.VMEM((5, NG, 2, 16, FOLD), i16),
+            pltpu.VMEM((5, NG, 2, 16, FOLD), i16),
+            pltpu.VMEM((5, NY, 2, 16, FOLD), i16),
+            pltpu.VMEM((5, NG, 2, 16, FOLD), i16),
             pltpu.VMEM((NZ, 16, 128), f32),
             dma((4,)),
             dma(()),
@@ -595,12 +610,12 @@
             dma(()),
             dma(()),
             dma(()),
-            dma((4,)),
-            dma((4,)),
-            dma((4,)),
-            dma((4,)),
-            dma((4,)),
-            dma((4,)),
+            dma((5,)),
+            dma((5,)),
+            dma((5,)),
+            dma((5,)),
+            dma((5,)),
+            dma((5,)),
             dma(()),
             dma(()),
         ],

time: 68 us -> 66.5 us (0.978)
  Pallas kernels: 62.2 us -> 60.7 us
    pallas_call x1, Pallas kernels: 62.2 us -> 60.7 us  [per_device(): pl.pallas_call(kernel, out_shape=(pltpu.VMEM((COLS, ROWS), f32), jax.Shap...]
where the time goes in v2:
time: 66.5 us; the launch traced here: 66.3 us
  Pallas kernels  60.7 us (91%)
  local copies, waits for them, and re-layouts  3.21 us (5%)
  between operations  2.4 us (4%)
    pallas_call x1, Pallas kernels, per_device(): pl.pallas_call(kernel, out_shape=(pltpu.VMEM((COLS, ROWS), f32), jax.Shap...  60.7 us
    unnamed x5, local copies, waits for them, and re-layouts  3.21 us

profile of v2, /device:TPU:1, one launch (start us, length us, event | category | flops | bytes accessed | tf_op | source)
XLA Modules:
  0.0 66.3 jit_solution(1553866241060833222)
XLA Ops:
  0.6 60.7 %shard_map.84 = (f32[672,1024]{1,0:T(8,128)S(1)}, f32[8,128]{1,0:T(8,128)}, f32[672,512]{1,0:T(8,128)S(1)}, f32[1,1]{1,0:T(1,128)}) custom-call(bf16[672,512]{1,0:T(8,128)(2,1)} %bitcast.12, f32[672,1024]{1,0:T(8,128)} %bitcast.11, f32[1,1024]{1,0:T(1,128)} %bitcast.13, s32[1,1024]{1,0:T(1,128)} %bitcast.14, s32[4,128]{1,0:T(4,128)} %bitcast.16), custom_call_target="tpu_custom_call" | custom-call | tf_op jit(solution)/shard_map/pallas_call | solution.py:564
  61.4 1.5 %copy.13 = f32[1024,672]{0,1:T(8,128)} copy(f32[1024,672]{0,1:T(8,128)S(1)} %bitcast.9) | data formatting | bytes 5505024
  62.9 0.0 copy-start
  62.9 1.1 %copy.14 = f32[512,672]{0,1:T(8,128)} copy(f32[512,672]{0,1:T(8,128)S(1)} %bitcast.10) | data formatting | bytes 2752512
  64.0 0.0 copy-done
  64.0 0.6 copy.15
Async XLA Ops:
  62.9 1.1 %copy-start = (f32[8,128]{1,0:T(8,128)S(1)}, f32[8,128]{1,0:T(8,128)}, u32[]{:S(2)}) copy-start(f32[8,128]{1,0:T(8,128)} %get-tuple-element.9) | copy-start | bytes 12292

commit v3 on v2

--- a/solution.py
+++ b/solution.py
@@ -42,10 +42,10 @@
 
 def kernel(
     hid_hbm, w_hbm, sc_hbm, fl_hbm, tg_hbm,
-    gw_out, gs_out, gh_out, loss_out,
-    w_v, sc1, fl1, tg4, ht_s, q_s, h_s, part, dl_s, tr_s, zt_s, own_s, root_s,
+    gw_out, gs_hbm, gh_out, loss_hbm,
+    gs_out, loss_out, w_v, sc1, fl1, tg4, ht_s, q_s, h_s, part, dl_s, tr_s, zt_s, own_s, root_s,
     rs_out, rs_in, ag_s, st_a, st_b, st_z, gh_s, a_out, a_in, b_buf, c_buf, f_buf,
-    w_sem, h_sem, small_sem,
+    w_sem, h_sem, small_sem, end_sem,
     rs_send, rs_recv, ag_send, ag_recv,
     sa_send, sa_recv, sb_send, sb_recv, sz_send, sz_recv,
     a_send, a_recv, b_send, b_recv, c_send, c_recv, f_send, f_recv,
@@ -495,9 +495,10 @@
         jnp.concatenate(rows_of + [jnp.zeros((120, 128), f32)], axis=0)
     )
 
+    stage_a(2)
     stage_a(1)
-    stage_a(2)
     stage_a(3)
+    stage_b(0)
     ag_last()
     form_squares(4)
     stage_a(4)
@@ -506,9 +507,9 @@
     def _(b):
         rows_grad(b)
 
-    stage_b(0)
+    stage_b(2)
     stage_b(1)
-    stage_b(2)
+    stage_c(0)
     stage_b(3)
     stage_b(4)
 
@@ -521,9 +522,8 @@
             src_ref=f_buf.at[w], dst_ref=f_buf.at[w], send_sem=f_send, recv_sem=f_recv,
             device_id=z_peer(j), device_id_type=MESH,
         ).start()
-    stage_c(0)
+    stage_c(2)
     stage_c(1)
-    stage_c(2)
     stage_c(3)
     stage_c(4)
     wait_bytes(f_buf.at[pl.ds(0, NZ - 1)], f_recv)
@@ -532,12 +532,20 @@
         tail += f_buf[i]
     gs_out[...] = tail[:8, :] * (1.0 / math.sqrt(D * 7.0))
     loss_out[...] = jnp.sum(tail[8:9, :], axis=1, keepdims=True)
+    end_copies = [
+        pltpu.make_async_copy(gs_out, gs_hbm, end_sem.at[0]),
+        pltpu.make_async_copy(loss_out, loss_hbm, end_sem.at[1]),
+    ]
+    for copy in end_copies:
+        copy.start()
     stage_d(0)
     stage_d(1)
     stage_d(2)
     stage_d(3)
     stage_d(4)
 
+    for copy in end_copies:
+        copy.wait()
     for k in range(len(groups)):
         n = len(groups[k])
         wait_bytes(a_out.at[k, pl.ds(0, NG - 1), pl.ds(0, n)], a_send.at[k])
@@ -570,8 +578,10 @@
             jax.ShapeDtypeStruct((1, 1), f32),
         ),
         in_specs=[anywhere] * 5,
-        out_specs=(vmem, vmem, vmem, vmem),
+        out_specs=(vmem, anywhere, vmem, anywhere),
         scratch_shapes=[
+            pltpu.VMEM((8, 128), f32),
+            pltpu.VMEM((1, 1), f32),
             pltpu.VMEM((COLS, ROWS), f32),
             pltpu.VMEM((1, ROWS), f32),
             pltpu.VMEM((1, ROWS), jnp.int32),
@@ -600,6 +610,7 @@
             dma((4,)),
             dma(()),
             dma((3,)),
+            dma((2,)),
             dma((2, 4, NS)),
             dma((2, 4, NS)),
             dma((2, 4, NS)),

time: 66.5 us -> 66.2 us (level)
  no operation moved by 1% of the time
where the time goes in v3:
time: 66.2 us; the launch traced here: 66.1 us
  Pallas kernels  60.5 us (91%)
  local copies, waits for them, and re-layouts  3.21 us (5%)
  between operations  2.4 us (4%)
    pallas_call x1, Pallas kernels, per_device(): pl.pallas_call(kernel, out_shape=(pltpu.VMEM((COLS, ROWS), f32), jax.Shap...  60.5 us
    unnamed x5, local copies, waits for them, and re-layouts  3.21 us

profile of v3, /device:TPU:1, one launch (start us, length us, event | category | flops | bytes accessed | tf_op | source)
XLA Modules:
  0.0 66.1 jit_solution(2983387857862172201)
XLA Ops:
  0.6 60.5 %shard_map.84 = (f32[672,1024]{1,0:T(8,128)S(1)}, f32[8,128]{1,0:T(8,128)}, f32[672,512]{1,0:T(8,128)S(1)}, f32[1,1]{1,0:T(1,128)}) custom-call(bf16[672,512]{1,0:T(8,128)(2,1)} %bitcast.12, f32[672,1024]{1,0:T(8,128)} %bitcast.11, f32[1,1024]{1,0:T(1,128)} %bitcast.13, s32[1,1024]{1,0:T(1,128)} %bitcast.14, s32[4,128]{1,0:T(4,128)} %bitcast.16), custom_call_target="tpu_custom_call" | custom-call | tf_op jit(solution)/shard_map/pallas_call | solution.py:572
  61.1 1.5 %copy.13 = f32[1024,672]{0,1:T(8,128)} copy(f32[1024,672]{0,1:T(8,128)S(1)} %bitcast.9) | data formatting | bytes 5505024
  62.7 0.0 copy-start
  62.7 1.1 %copy.14 = f32[512,672]{0,1:T(8,128)} copy(f32[512,672]{0,1:T(8,128)S(1)} %bitcast.10) | data formatting | bytes 2752512
  63.7 0.0 copy-done
  63.7 0.6 copy.15
Async XLA Ops:
  62.7 1.1 %copy-start = (f32[8,128]{1,0:T(8,128)S(1)}, f32[8,128]{1,0:T(8,128)}, u32[]{:S(2)}) copy-start(f32[8,128]{1,0:T(8,128)} %get-tuple-element.9) | copy-start | bytes 12292

commit v4 on v3

--- a/solution.py
+++ b/solution.py
@@ -342,8 +342,9 @@
         root = codes.astype(i32).astype(f32) + ROOT_MID
         part[block_rows(shift), :] = root * root
 
-    groups = [(0,), (-1, 1), (-2, 2), (-3, 3), (4,)]
-    modes = ["x", "x", "y", "y", "x"]
+    groups = [(0,), (-1, 1), (-3, -2, 2, 3), (4,)]
+    modes = ["x", "x", "y", "x"]
+    units = [(), (0,), (1, 2), (3,)]
     nt = (((1,), (1,)), ((), ()))
 
     def fold(x):
@@ -432,8 +433,8 @@
         wait_bytes(c_buf.at[k, pl.ds(0, NG - 1), pl.ds(0, n)], c_recv.at[k])
         for s, shift in enumerate(groups[k]):
             gh_s[block_rows(shift), :] = unfold(c_buf[k, :, s])
-        if k > 0:
-            pair = unit_lanes(k - 1)
+        for i in units[k]:
+            pair = unit_lanes(i)
             gh_out[:, pair] = jnp.transpose(gh_s[pair, :])[:COLS, :]
 
     GB = 256
@@ -497,21 +498,19 @@
 
     stage_a(2)
     stage_a(1)
-    stage_a(3)
     stage_b(0)
     ag_last()
     form_squares(4)
-    stage_a(4)
+    stage_a(3)
 
     @pl.loop(0, 2)
     def _(b):
         rows_grad(b)
 
-    stage_b(2)
     stage_b(1)
     stage_c(0)
+    stage_b(2)
     stage_b(3)
-    stage_b(4)
 
     @pl.loop(2, 4)
     def _(b):
@@ -522,10 +521,9 @@
             src_ref=f_buf.at[w], dst_ref=f_buf.at[w], send_sem=f_send, recv_sem=f_recv,
             device_id=z_peer(j), device_id_type=MESH,
         ).start()
+    stage_c(1)
     stage_c(2)
-    stage_c(1)
     stage_c(3)
-    stage_c(4)
     wait_bytes(f_buf.at[pl.ds(0, NZ - 1)], f_recv)
     tail = f_buf[0]
     for i in range(1, NZ):
@@ -542,7 +540,6 @@
     stage_d(1)
     stage_d(2)
     stage_d(3)
-    stage_d(4)
 
     for copy in end_copies:
         copy.wait()
@@ -602,10 +599,10 @@
             pltpu.VMEM((NY, 8, 128), f32),
             pltpu.VMEM((NZ, 8, 128), f32),
             pltpu.VMEM((512, PAD), f32),
-            pltpu.VMEM((5, NG, 2, 16, FOLD), i16),
-            pltpu.VMEM((5, NG, 2, 16, FOLD), i16),
-            pltpu.VMEM((5, NY, 2, 16, FOLD), i16),
-            pltpu.VMEM((5, NG, 2, 16, FOLD), i16),
+            pltpu.VMEM((4, NG, 4, 16, FOLD), i16),
+            pltpu.VMEM((4, NG, 4, 16, FOLD), i16),
+            pltpu.VMEM((4, NY, 4, 16, FOLD), i16),
+            pltpu.VMEM((4, NG, 4, 16, FOLD), i16),
             pltpu.VMEM((NZ, 16, 128), f32),
             dma((4,)),
             dma(()),
@@ -621,12 +618,12 @@
             dma(()),
             dma(()),
             dma(()),
-            dma((5,)),
-            dma((5,)),
-            dma((5,)),
-            dma((5,)),
-            dma((5,)),
-            dma((5,)),
+            dma((4,)),
+            dma((4,)),
+            dma((4,)),
+            dma((4,)),
+            dma((4,)),
+            dma((4,)),
             dma(()),
             dma(()),
         ],

time: 66.2 us -> 68.2 us (1.030)
  Pallas kernels: 60.5 us -> 62.5 us
    pallas_call x1, Pallas kernels: 60.5 us -> 62.5 us  [per_device(): pl.pallas_call(kernel, out_shape=(pltpu.VMEM((COLS, ROWS), f32), jax.Shap...]
where the time goes in v4:
time: 68.2 us; the launch traced here: 68.1 us
  Pallas kernels  62.5 us (92%)
  local copies, waits for them, and re-layouts  3.21 us (5%)
  between operations  2.4 us (4%)
    pallas_call x1, Pallas kernels, per_device(): pl.pallas_call(kernel, out_shape=(pltpu.VMEM((COLS, ROWS), f32), jax.Shap...  62.5 us
    unnamed x5, local copies, waits for them, and re-layouts  3.21 us

profile of v4, /device:TPU:1, one launch (start us, length us, event | category | flops | bytes accessed | tf_op | source)
XLA Modules:
  0.0 68.1 jit_solution(11928505343765826435)
XLA Ops:
  0.6 62.5 %shard_map.84 = (f32[672,1024]{1,0:T(8,128)S(1)}, f32[8,128]{1,0:T(8,128)}, f32[672,512]{1,0:T(8,128)S(1)}, f32[1,1]{1,0:T(1,128)}) custom-call(bf16[672,512]{1,0:T(8,128)(2,1)} %bitcast.12, f32[672,1024]{1,0:T(8,128)} %bitcast.11, f32[1,1024]{1,0:T(1,128)} %bitcast.13, s32[1,1024]{1,0:T(1,128)} %bitcast.14, s32[4,128]{1,0:T(4,128)} %bitcast.16), custom_call_target="tpu_custom_call" | custom-call | tf_op jit(solution)/shard_map/pallas_call | solution.py:569
  63.2 1.5 %copy.13 = f32[1024,672]{0,1:T(8,128)} copy(f32[1024,672]{0,1:T(8,128)S(1)} %bitcast.9) | data formatting | bytes 5505024
  64.7 0.0 copy-start
  64.7 1.1 %copy.14 = f32[512,672]{0,1:T(8,128)} copy(f32[512,672]{0,1:T(8,128)S(1)} %bitcast.10) | data formatting | bytes 2752512
  65.8 0.0 copy-done
  65.8 0.6 copy.15
Async XLA Ops:
  64.7 1.1 %copy-start = (f32[8,128]{1,0:T(8,128)S(1)}, f32[8,128]{1,0:T(8,128)}, u32[]{:S(2)}) copy-start(f32[8,128]{1,0:T(8,128)} %get-tuple-element.9) | copy-start | bytes 12292
